TPU v7x, 32 devices: a whole 2x2x4 slice. The times are simulated.
32 devices in a mesh: kv: 8 (over z, x), head: 4 (over y, core).
Axes of the slice: x: 2, y: 2, z: 4, core: 2. Of those that a mesh axis runs over, the one named last changes fastest.
Arguments:
- query: bfloat16 [2, 40, 128, 128], P(None, None, 'head'), may hold values from -16 to 16
- key_cache: bfloat16 [2, 8, 65536, 128], P(None, 'head', 'kv'), may hold values from -6 to 6
- value_cache: bfloat16 [2, 8, 65536, 128], P(None, 'head', 'kv'), may hold values from -6 to 6
- draft_keys: bfloat16 [2, 8, 40, 128], P(None, 'head'), may hold values from -12 to 12
- draft_values: bfloat16 [2, 8, 40, 128], P(None, 'head'), may hold values from -6 to 6
- lengths: int32 [2], replicated, may hold values from 8192 to 65536, as said below
- out_weight: bfloat16 [16384, 16384], P('head', 'kv'), may hold values from -0.1875 to 0.1875
Outputs:
- mixed: bfloat16 [2, 40, 16384], P(None, None, ('kv', 'head'))
Inputs may be any that keep to these rules, and one draw needn't show every extreme that they name: `lengths`: one request has exactly 65536 cached positions.
All inputs are finite; a program needn't handle non-finite values.
Results may differ from a plain program's by a relative error of at most 0.0055.
Values may be sent and summed in bfloat16 or wider, within the bound.
A program may use at most 128 MiB of HBM per device.

v0:
```python
import math

import jax
import jax.numpy as jnp
from jax import lax
from jax.sharding import PartitionSpec as P

masked_score = -1e30


def per_device(query, key_cache, value_cache, draft_keys, draft_values, lengths, out_weight):
    batch, draft, qheads, head_width = query.shape
    kv_heads = key_cache.shape[1]
    local_span = key_cache.shape[2]
    group = qheads // kv_heads
    kv_count = lax.axis_size("kv")
    kv_index = lax.axis_index("kv")
    score_scale = 1.0 / math.sqrt(head_width)
    queries = query.reshape(batch, draft, kv_heads, group, head_width)
    block_rows = min(512, local_span)
    blocks = local_span // block_rows
    start_pos = kv_index * local_span

    def absorb(state, scores, live, values):
        run_max, run_sum, mixture = state
        new_max = jnp.maximum(run_max, jnp.max(scores, axis=-1))
        weights = jnp.where(live, jnp.exp(scores - new_max[..., None]), 0.0)
        factor = jnp.exp(run_max - new_max)
        run_sum = run_sum * factor + jnp.sum(weights, axis=-1)
        mixture = mixture * factor[..., None] + jnp.einsum(
            "bkjgt,bktd->bkjgd",
            weights,
            values.astype(jnp.float32),
            preferred_element_type=jnp.float32,
        )
        return (new_max, run_sum, mixture)

    def cache_block(step_index, state):
        first_row = step_index * block_rows
        key_block = lax.dynamic_slice_in_dim(key_cache, first_row, block_rows, 2)
        value_block = lax.dynamic_slice_in_dim(value_cache, first_row, block_rows, 2)
        scores = (
            jnp.einsum("bjkgd,bktd->bkjgt", queries, key_block, preferred_element_type=jnp.float32)
            * score_scale
        )
        positions = start_pos + first_row + jnp.arange(block_rows)
        live = (positions[None, :] < lengths[:, None])[:, None, None, None, :]
        scores = jnp.where(live, scores, masked_score)
        return absorb(state, scores, live, value_block)

    stat_shape = (batch, kv_heads, draft, group)
    state = (
        jnp.full(stat_shape, masked_score, jnp.float32),
        jnp.zeros(stat_shape, jnp.float32),
        jnp.zeros(stat_shape + (head_width,), jnp.float32),
    )
    state = lax.fori_loop(0, blocks, cache_block, state)
    draft_scores = (
        jnp.einsum("bjkgd,bkid->bkjgi", queries, draft_keys, preferred_element_type=jnp.float32)
        * score_scale
    )
    causal = jnp.arange(draft)[None, :] <= jnp.arange(draft)[:, None]
    draft_live = jnp.logical_and(causal, kv_index == kv_count - 1)[None, None, :, None, :]
    draft_scores = jnp.where(draft_live, draft_scores, masked_score)
    run_max, run_sum, mixture = absorb(state, draft_scores, draft_live, draft_values)
    row_count = batch * draft
    mixture = jnp.transpose(mixture, (0, 2, 1, 3, 4)).reshape(row_count, qheads, head_width)
    run_max = jnp.transpose(run_max, (0, 2, 1, 3)).reshape(row_count, qheads)
    run_sum = jnp.transpose(run_sum, (0, 2, 1, 3)).reshape(row_count, qheads)
    feat_dev = qheads * head_width // kv_count
    unit_width = min(feat_dev, head_width)
    unit_count = head_width // unit_width
    unit_dev = feat_dev // unit_width
    sent_mix = mixture.reshape(row_count, kv_count, feat_dev)
    sent_max = jnp.repeat(run_max, unit_count, axis=1).reshape(row_count, kv_count, unit_dev)
    sent_sum = jnp.repeat(run_sum, unit_count, axis=1).reshape(row_count, kv_count, unit_dev)
    got_mix, got_max, got_sum = (
        lax.all_to_all(sent_mix, "kv", split_axis=1, concat_axis=1, tiled=True),
        lax.all_to_all(sent_max, "kv", split_axis=1, concat_axis=1, tiled=True),
        lax.all_to_all(sent_sum, "kv", split_axis=1, concat_axis=1, tiled=True),
    )
    peak = jnp.max(got_max, axis=1)
    factor = jnp.exp(got_max - peak[:, None, :])
    total = jnp.sum(got_sum * factor, axis=1)
    merged = jnp.sum(
        got_mix.reshape(row_count, kv_count, unit_dev, unit_width) * factor[..., None], axis=1
    )
    attention = (merged / total[..., None]).reshape(row_count, feat_dev).astype(jnp.bfloat16)
    partial_value = jnp.dot(
        lax.all_gather(attention, "kv", axis=1, tiled=True),
        out_weight,
        preferred_element_type=jnp.float32,
    )
    mixed = lax.psum_scatter(partial_value, "head", scatter_dimension=1, tiled=True).astype(
        jnp.bfloat16
    )
    return mixed.reshape(batch, draft, -1)


def solution(mesh):
    in_specs = (
        P(None, None, "head", None),
        P(None, "head", "kv", None),
        P(None, "head", "kv", None),
        P(None, "head", None, None),
        P(None, "head", None, None),
        P(),
        P("head", "kv"),
    )
    out_specs = P(None, None, ("kv", "head"))
    return jax.shard_map(
        per_device, mesh=mesh, in_specs=in_specs, out_specs=out_specs, check_vma=False
    )
```

profile of v0, /device:TPU:1, one launch (start us, length us, event | category | flops | bytes accessed | tf_op | source)
XLA Modules:
  0.0 325.4 jit_solution(4562720456418302520)
XLA Ops:
  7.9 186.2 %while.18 = (s32[]{:T(128)}, f32[2,2,40,16]{2,3,1,0:T(8,128)S(1)}, f32[2,2,40,16]{2,3,1,0:T(8,128)S(1)}, f32[2,2,40,16,128]{4,2,3,1,0:T(8,128)S(1)}, s32[]{:T(12...) while((s32[]{:T(128)}, f32[2,2,40,16]{2,3,1,0:T(8,128)S(1)}, ...), condition=%wide.region_3.4_spmd.clone, body=%wide.region_0.3_spmd.clone.sunk | while | flops 687814656 | bytes 41245936 | solution.py:57
  8.0 4.3 %bitcast_reduce_fusion.2 = (f32[2,2,40,16]{2,3,1,0:T(8,128)S(1)}, f32[2,2,512,40,16]{2,3,4,1,0:T(8,128)}) fusion(pred[2,512]{1,0:T(4,128)(4,1)S(1)} %broadcast_compare_fusion.2, bf16[2,40,2,16,128]{4,1,3,2,0:T(8,128)(2,1)S(1)} %get-tuple-element.318, bf16[2,2,8192,128]{3,2,1,0:T(8,128)(2,1)} %get-tuple-element.317, s32[]{:T(128)S(6)} %select_n.71), kind=kOutput, calls=%fused_computation.1.clone.1 | convolution fusion | flops 339473920 | bytes 6433796 | tf_op jit(solution)/shard_map/while/body/eval_jaxpr/bjkgd,bktd->bkjgt/dot_general | solution.py:43
  12.3 3.7 %fusion.51 = f32[2,2,40,16]{2,3,1,0:T(8,128)S(1)} fusion(f32[2,2,512,40,16]{2,3,4,1,0:T(8,128)} %get-tuple-element.282, f32[2,2,40,16]{2,3,1,0:T(8,128)S(1)} %select_maximum_fusion.2, pred[2,512]{1,0:T(4,128)(4,1)S(1)} %broadcast_compare_fusion.2), kind=kLoop, calls=%fused_computation.6.clone.1 | loop fusion | flops 6551040 | bytes 5264384 | tf_op jit(solution)/shard_map/while/body/eval_jaxpr/reduce_sum | solution.py:29
  19.7 4.3 %bitcast_reduce_fusion.2 = (f32[2,2,40,16]{2,3,1,0:T(8,128)S(1)}, f32[2,2,512,40,16]{2,3,4,1,0:T(8,128)}) fusion(pred[2,512]{1,0:T(4,128)(4,1)S(1)} %broadcast_compare_fusion.2, bf16[2,40,2,16,128]{4,1,3,2,0:T(8,128)(2,1)S(1)} %get-tuple-element.318, bf16[2,2,8192,128]{3,2,1,0:T(8,128)(2,1)} %get-tuple-element.317, s32[]{:T(128)S(6)} %select_n.71), kind=kOutput, calls=%fused_computation.1.clone.1 | convolution fusion | flops 339473920 | bytes 6433796 | tf_op jit(solution)/shard_map/while/body/eval_jaxpr/bjkgd,bktd->bkjgt/dot_general | solution.py:43
  31.3 4.3 %bitcast_reduce_fusion.2 = (f32[2,2,40,16]{2,3,1,0:T(8,128)S(1)}, f32[2,2,512,40,16]{2,3,4,1,0:T(8,128)}) fusion(pred[2,512]{1,0:T(4,128)(4,1)S(1)} %broadcast_compare_fusion.2, bf16[2,40,2,16,128]{4,1,3,2,0:T(8,128)(2,1)S(1)} %get-tuple-element.318, bf16[2,2,8192,128]{3,2,1,0:T(8,128)(2,1)} %get-tuple-element.317, s32[]{:T(128)S(6)} %select_n.71), kind=kOutput, calls=%fused_computation.1.clone.1 | convolution fusion | flops 339473920 | bytes 6433796 | tf_op jit(solution)/shard_map/while/body/eval_jaxpr/bjkgd,bktd->bkjgt/dot_general | solution.py:43
  35.6 3.7 %fusion.51 = f32[2,2,40,16]{2,3,1,0:T(8,128)S(1)} fusion(f32[2,2,512,40,16]{2,3,4,1,0:T(8,128)} %get-tuple-element.282, f32[2,2,40,16]{2,3,1,0:T(8,128)S(1)} %select_maximum_fusion.2, pred[2,512]{1,0:T(4,128)(4,1)S(1)} %broadcast_compare_fusion.2), kind=kLoop, calls=%fused_computation.6.clone.1 | loop fusion | flops 6551040 | bytes 5264384 | tf_op jit(solution)/shard_map/while/body/eval_jaxpr/reduce_sum | solution.py:29
  43.0 4.3 %bitcast_reduce_fusion.2 = (f32[2,2,40,16]{2,3,1,0:T(8,128)S(1)}, f32[2,2,512,40,16]{2,3,4,1,0:T(8,128)}) fusion(pred[2,512]{1,0:T(4,128)(4,1)S(1)} %broadcast_compare_fusion.2, bf16[2,40,2,16,128]{4,1,3,2,0:T(8,128)(2,1)S(1)} %get-tuple-element.318, bf16[2,2,8192,128]{3,2,1,0:T(8,128)(2,1)} %get-tuple-element.317, s32[]{:T(128)S(6)} %select_n.71), kind=kOutput, calls=%fused_computation.1.clone.1 | convolution fusion | flops 339473920 | bytes 6433796 | tf_op jit(solution)/shard_map/while/body/eval_jaxpr/bjkgd,bktd->bkjgt/dot_general | solution.py:43
  47.3 3.7 %fusion.51 = f32[2,2,40,16]{2,3,1,0:T(8,128)S(1)} fusion(f32[2,2,512,40,16]{2,3,4,1,0:T(8,128)} %get-tuple-element.282, f32[2,2,40,16]{2,3,1,0:T(8,128)S(1)} %select_maximum_fusion.2, pred[2,512]{1,0:T(4,128)(4,1)S(1)} %broadcast_compare_fusion.2), kind=kLoop, calls=%fused_computation.6.clone.1 | loop fusion | flops 6551040 | bytes 5264384 | tf_op jit(solution)/shard_map/while/body/eval_jaxpr/reduce_sum | solution.py:29
  54.6 4.3 %bitcast_reduce_fusion.2 = (f32[2,2,40,16]{2,3,1,0:T(8,128)S(1)}, f32[2,2,512,40,16]{2,3,4,1,0:T(8,128)}) fusion(pred[2,512]{1,0:T(4,128)(4,1)S(1)} %broadcast_compare_fusion.2, bf16[2,40,2,16,128]{4,1,3,2,0:T(8,128)(2,1)S(1)} %get-tuple-element.318, bf16[2,2,8192,128]{3,2,1,0:T(8,128)(2,1)} %get-tuple-element.317, s32[]{:T(128)S(6)} %select_n.71), kind=kOutput, calls=%fused_computation.1.clone.1 | convolution fusion | flops 339473920 | bytes 6433796 | tf_op jit(solution)/shard_map/while/body/eval_jaxpr/bjkgd,bktd->bkjgt/dot_general | solution.py:43
  58.9 3.7 %fusion.51 = f32[2,2,40,16]{2,3,1,0:T(8,128)S(1)} fusion(f32[2,2,512,40,16]{2,3,4,1,0:T(8,128)} %get-tuple-element.282, f32[2,2,40,16]{2,3,1,0:T(8,128)S(1)} %select_maximum_fusion.2, pred[2,512]{1,0:T(4,128)(4,1)S(1)} %broadcast_compare_fusion.2), kind=kLoop, calls=%fused_computation.6.clone.1 | loop fusion | flops 6551040 | bytes 5264384 | tf_op jit(solution)/shard_map/while/body/eval_jaxpr/reduce_sum | solution.py:29
  66.2 4.3 %bitcast_reduce_fusion.2 = (f32[2,2,40,16]{2,3,1,0:T(8,128)S(1)}, f32[2,2,512,40,16]{2,3,4,1,0:T(8,128)}) fusion(pred[2,512]{1,0:T(4,128)(4,1)S(1)} %broadcast_compare_fusion.2, bf16[2,40,2,16,128]{4,1,3,2,0:T(8,128)(2,1)S(1)} %get-tuple-element.318, bf16[2,2,8192,128]{3,2,1,0:T(8,128)(2,1)} %get-tuple-element.317, s32[]{:T(128)S(6)} %select_n.71), kind=kOutput, calls=%fused_computation.1.clone.1 | convolution fusion | flops 339473920 | bytes 6433796 | tf_op jit(solution)/shard_map/while/body/eval_jaxpr/bjkgd,bktd->bkjgt/dot_general | solution.py:43
  70.5 3.7 %fusion.51 = f32[2,2,40,16]{2,3,1,0:T(8,128)S(1)} fusion(f32[2,2,512,40,16]{2,3,4,1,0:T(8,128)} %get-tuple-element.282, f32[2,2,40,16]{2,3,1,0:T(8,128)S(1)} %select_maximum_fusion.2, pred[2,512]{1,0:T(4,128)(4,1)S(1)} %broadcast_compare_fusion.2), kind=kLoop, calls=%fused_computation.6.clone.1 | loop fusion | flops 6551040 | bytes 5264384 | tf_op jit(solution)/shard_map/while/body/eval_jaxpr/reduce_sum | solution.py:29
  77.9 4.3 %bitcast_reduce_fusion.2 = (f32[2,2,40,16]{2,3,1,0:T(8,128)S(1)}, f32[2,2,512,40,16]{2,3,4,1,0:T(8,128)}) fusion(pred[2,512]{1,0:T(4,128)(4,1)S(1)} %broadcast_compare_fusion.2, bf16[2,40,2,16,128]{4,1,3,2,0:T(8,128)(2,1)S(1)} %get-tuple-element.318, bf16[2,2,8192,128]{3,2,1,0:T(8,128)(2,1)} %get-tuple-element.317, s32[]{:T(128)S(6)} %select_n.71), kind=kOutput, calls=%fused_computation.1.clone.1 | convolution fusion | flops 339473920 | bytes 6433796 | tf_op jit(solution)/shard_map/while/body/eval_jaxpr/bjkgd,bktd->bkjgt/dot_general | solution.py:43
  82.2 3.7 %fusion.51 = f32[2,2,40,16]{2,3,1,0:T(8,128)S(1)} fusion(f32[2,2,512,40,16]{2,3,4,1,0:T(8,128)} %get-tuple-element.282, f32[2,2,40,16]{2,3,1,0:T(8,128)S(1)} %select_maximum_fusion.2, pred[2,512]{1,0:T(4,128)(4,1)S(1)} %broadcast_compare_fusion.2), kind=kLoop, calls=%fused_computation.6.clone.1 | loop fusion | flops 6551040 | bytes 5264384 | tf_op jit(solution)/shard_map/while/body/eval_jaxpr/reduce_sum | solution.py:29
  89.5 4.3 %bitcast_reduce_fusion.2 = (f32[2,2,40,16]{2,3,1,0:T(8,128)S(1)}, f32[2,2,512,40,16]{2,3,4,1,0:T(8,128)}) fusion(pred[2,512]{1,0:T(4,128)(4,1)S(1)} %broadcast_compare_fusion.2, bf16[2,40,2,16,128]{4,1,3,2,0:T(8,128)(2,1)S(1)} %get-tuple-element.318, bf16[2,2,8192,128]{3,2,1,0:T(8,128)(2,1)} %get-tuple-element.317, s32[]{:T(128)S(6)} %select_n.71), kind=kOutput, calls=%fused_computation.1.clone.1 | convolution fusion | flops 339473920 | bytes 6433796 | tf_op jit(solution)/shard_map/while/body/eval_jaxpr/bjkgd,bktd->bkjgt/dot_general | solution.py:43
  93.8 3.7 %fusion.51 = f32[2,2,40,16]{2,3,1,0:T(8,128)S(1)} fusion(f32[2,2,512,40,16]{2,3,4,1,0:T(8,128)} %get-tuple-element.282, f32[2,2,40,16]{2,3,1,0:T(8,128)S(1)} %select_maximum_fusion.2, pred[2,512]{1,0:T(4,128)(4,1)S(1)} %broadcast_compare_fusion.2), kind=kLoop, calls=%fused_computation.6.clone.1 | loop fusion | flops 6551040 | bytes 5264384 | tf_op jit(solution)/shard_map/while/body/eval_jaxpr/reduce_sum | solution.py:29
  101.1 4.3 %bitcast_reduce_fusion.2 = (f32[2,2,40,16]{2,3,1,0:T(8,128)S(1)}, f32[2,2,512,40,16]{2,3,4,1,0:T(8,128)}) fusion(pred[2,512]{1,0:T(4,128)(4,1)S(1)} %broadcast_compare_fusion.2, bf16[2,40,2,16,128]{4,1,3,2,0:T(8,128)(2,1)S(1)} %get-tuple-element.318, bf16[2,2,8192,128]{3,2,1,0:T(8,128)(2,1)} %get-tuple-element.317, s32[]{:T(128)S(6)} %select_n.71), kind=kOutput, calls=%fused_computation.1.clone.1 | convolution fusion | flops 339473920 | bytes 6433796 | tf_op jit(solution)/shard_map/while/body/eval_jaxpr/bjkgd,bktd->bkjgt/dot_general | solution.py:43
  105.4 3.7 %fusion.51 = f32[2,2,40,16]{2,3,1,0:T(8,128)S(1)} fusion(f32[2,2,512,40,16]{2,3,4,1,0:T(8,128)} %get-tuple-element.282, f32[2,2,40,16]{2,3,1,0:T(8,128)S(1)} %select_maximum_fusion.2, pred[2,512]{1,0:T(4,128)(4,1)S(1)} %broadcast_compare_fusion.2), kind=kLoop, calls=%fused_computation.6.clone.1 | loop fusion | flops 6551040 | bytes 5264384 | tf_op jit(solution)/shard_map/while/body/eval_jaxpr/reduce_sum | solution.py:29
  112.8 4.3 %bitcast_reduce_fusion.2 = (f32[2,2,40,16]{2,3,1,0:T(8,128)S(1)}, f32[2,2,512,40,16]{2,3,4,1,0:T(8,128)}) fusion(pred[2,512]{1,0:T(4,128)(4,1)S(1)} %broadcast_compare_fusion.2, bf16[2,40,2,16,128]{4,1,3,2,0:T(8,128)(2,1)S(1)} %get-tuple-element.318, bf16[2,2,8192,128]{3,2,1,0:T(8,128)(2,1)} %get-tuple-element.317, s32[]{:T(128)S(6)} %select_n.71), kind=kOutput, calls=%fused_computation.1.clone.1 | convolution fusion | flops 339473920 | bytes 6433796 | tf_op jit(solution)/shard_map/while/body/eval_jaxpr/bjkgd,bktd->bkjgt/dot_general | solution.py:43
  117.1 3.7 %fusion.51 = f32[2,2,40,16]{2,3,1,0:T(8,128)S(1)} fusion(f32[2,2,512,40,16]{2,3,4,1,0:T(8,128)} %get-tuple-element.282, f32[2,2,40,16]{2,3,1,0:T(8,128)S(1)} %select_maximum_fusion.2, pred[2,512]{1,0:T(4,128)(4,1)S(1)} %broadcast_compare_fusion.2), kind=kLoop, calls=%fused_computation.6.clone.1 | loop fusion | flops 6551040 | bytes 5264384 | tf_op jit(solution)/shard_map/while/body/eval_jaxpr/reduce_sum | solution.py:29
  124.4 4.3 %bitcast_reduce_fusion.2 = (f32[2,2,40,16]{2,3,1,0:T(8,128)S(1)}, f32[2,2,512,40,16]{2,3,4,1,0:T(8,128)}) fusion(pred[2,512]{1,0:T(4,128)(4,1)S(1)} %broadcast_compare_fusion.2, bf16[2,40,2,16,128]{4,1,3,2,0:T(8,128)(2,1)S(1)} %get-tuple-element.318, bf16[2,2,8192,128]{3,2,1,0:T(8,128)(2,1)} %get-tuple-element.317, s32[]{:T(128)S(6)} %select_n.71), kind=kOutput, calls=%fused_computation.1.clone.1 | convolution fusion | flops 339473920 | bytes 6433796 | tf_op jit(solution)/shard_map/while/body/eval_jaxpr/bjkgd,bktd->bkjgt/dot_general | solution.py:43
  136.1 4.3 %bitcast_reduce_fusion.2 = (f32[2,2,40,16]{2,3,1,0:T(8,128)S(1)}, f32[2,2,512,40,16]{2,3,4,1,0:T(8,128)}) fusion(pred[2,512]{1,0:T(4,128)(4,1)S(1)} %broadcast_compare_fusion.2, bf16[2,40,2,16,128]{4,1,3,2,0:T(8,128)(2,1)S(1)} %get-tuple-element.318, bf16[2,2,8192,128]{3,2,1,0:T(8,128)(2,1)} %get-tuple-element.317, s32[]{:T(128)S(6)} %select_n.71), kind=kOutput, calls=%fused_computation.1.clone.1 | convolution fusion | flops 339473920 | bytes 6433796 | tf_op jit(solution)/shard_map/while/body/eval_jaxpr/bjkgd,bktd->bkjgt/dot_general | solution.py:43
  147.7 4.3 %bitcast_reduce_fusion.2 = (f32[2,2,40,16]{2,3,1,0:T(8,128)S(1)}, f32[2,2,512,40,16]{2,3,4,1,0:T(8,128)}) fusion(pred[2,512]{1,0:T(4,128)(4,1)S(1)} %broadcast_compare_fusion.2, bf16[2,40,2,16,128]{4,1,3,2,0:T(8,128)(2,1)S(1)} %get-tuple-element.318, bf16[2,2,8192,128]{3,2,1,0:T(8,128)(2,1)} %get-tuple-element.317, s32[]{:T(128)S(6)} %select_n.71), kind=kOutput, calls=%fused_computation.1.clone.1 | convolution fusion | flops 339473920 | bytes 6433796 | tf_op jit(solution)/shard_map/while/body/eval_jaxpr/bjkgd,bktd->bkjgt/dot_general | solution.py:43
  159.3 4.3 %bitcast_reduce_fusion.2 = (f32[2,2,40,16]{2,3,1,0:T(8,128)S(1)}, f32[2,2,512,40,16]{2,3,4,1,0:T(8,128)}) fusion(pred[2,512]{1,0:T(4,128)(4,1)S(1)} %broadcast_compare_fusion.2, bf16[2,40,2,16,128]{4,1,3,2,0:T(8,128)(2,1)S(1)} %get-tuple-element.318, bf16[2,2,8192,128]{3,2,1,0:T(8,128)(2,1)} %get-tuple-element.317, s32[]{:T(128)S(6)} %select_n.71), kind=kOutput, calls=%fused_computation.1.clone.1 | convolution fusion | flops 339473920 | bytes 6433796 | tf_op jit(solution)/shard_map/while/body/eval_jaxpr/bjkgd,bktd->bkjgt/dot_general | solution.py:43
  171.0 4.3 %bitcast_reduce_fusion.2 = (f32[2,2,40,16]{2,3,1,0:T(8,128)S(1)}, f32[2,2,512,40,16]{2,3,4,1,0:T(8,128)}) fusion(pred[2,512]{1,0:T(4,128)(4,1)S(1)} %broadcast_compare_fusion.2, bf16[2,40,2,16,128]{4,1,3,2,0:T(8,128)(2,1)S(1)} %get-tuple-element.318, bf16[2,2,8192,128]{3,2,1,0:T(8,128)(2,1)} %get-tuple-element.317, s32[]{:T(128)S(6)} %select_n.71), kind=kOutput, calls=%fused_computation.1.clone.1 | convolution fusion | flops 339473920 | bytes 6433796 | tf_op jit(solution)/shard_map/while/body/eval_jaxpr/bjkgd,bktd->bkjgt/dot_general | solution.py:43
  182.6 4.3 %bitcast_reduce_fusion.2 = (f32[2,2,40,16]{2,3,1,0:T(8,128)S(1)}, f32[2,2,512,40,16]{2,3,4,1,0:T(8,128)}) fusion(pred[2,512]{1,0:T(4,128)(4,1)S(1)} %broadcast_compare_fusion.2, bf16[2,40,2,16,128]{4,1,3,2,0:T(8,128)(2,1)S(1)} %get-tuple-element.318, bf16[2,2,8192,128]{3,2,1,0:T(8,128)(2,1)} %get-tuple-element.317, s32[]{:T(128)S(6)} %select_n.71), kind=kOutput, calls=%fused_computation.1.clone.1 | convolution fusion | flops 339473920 | bytes 6433796 | tf_op jit(solution)/shard_map/while/body/eval_jaxpr/bjkgd,bktd->bkjgt/dot_general | solution.py:43
  197.7 6.3 %all-to-all-start.2 = ((f32[80,8,4]{0,2,1:T(4,128)}), f32[80,8,4]{0,2,1:T(4,128)S(1)}, u32[]{:S(2)}, u32[]{:S(2)}) async-start(f32[80,8,4]{0,2,1:T(4,128)} %reshape_reshape_broadcast_in_dim_reshape.7), calls=%async_computation.2 | async-start | bytes 32768 | tf_op jit(solution)/shard_map/all_to_all | solution.py:80
  204.8 4.6 %all-to-all-done.2 = f32[80,8,4]{0,2,1:T(4,128)S(1)} async-done(((f32[80,8,4]{0,2,1:T(4,128)}), f32[80,8,4]{0,2,1:T(4,128)S(1)}, u32[]{:S(2)}, u32[]{:S(2)}) %all-to-all-start.2) | async-done | bytes 10272 | tf_op jit(solution)/shard_map/all_to_all | solution.py:80
  225.6 25.3 %all-to-all-done = f32[80,8,512]{2,0,1:T(8,128)S(1)} async-done(((f32[80,8,512]{2,0,1:T(8,128)}), f32[80,8,512]{2,0,1:T(8,128)S(1)}, u32[]{:S(2)}, u32[]{:S(2)}) %all-to-all-start) | async-done | bytes 1310752 | tf_op jit(solution)/shard_map/all_to_all | solution.py:78
  251.3 26.8 %all_gather.3 = bf16[80,4096]{1,0:T(8,128)(2,1)S(1)} all-gather(bf16[80,512]{1,0:T(8,128)(2,1)S(1)} %fusion.32), channel_id=1, replica_groups=mesh['kv'=8,'head'=4] {'kv'}, dimensions={1}, use_global_device_ids=true | all-gather | bytes 737280 | tf_op jit(solution)/shard_map/all_gather | solution.py:90
  278.1 9.6 %fusion.38 = f32[80,2048]{1,0:T(8,128)} fusion(bf16[80,4096]{1,0:T(8,128)(2,1)S(1)} %all_gather.3, bf16[4096,2048]{1,0:T(8,128)(2,1)} %param.15), kind=kOutput, calls=%fused_computation.55 | convolution fusion | flops 1342177280 | bytes 18087936 | tf_op jit(solution)/shard_map/dot_general | solution.py:89
  287.8 29.2 %reduce-scatter.2.cloned.1.call-done = f32[80,512]{1,0:T(8,128)} async-done(((f32[80,2048]{1,0:T(8,128)}), f32[80,512]{1,0:T(8,128)}) %reduce-scatter.2.cloned.1.call-update) | async-done | bytes 163856 | tf_op jit(solution)/shard_map/reduce_scatter | solution.py:94
  (175 shorter events, 107.3 us)
Async XLA Ops:
  6.5 206.2 %copy-start = (bf16[2,2,40,128]{3,2,1,0:T(8,128)(2,1)S(1)}, bf16[2,2,40,128]{3,2,1,0:T(8,128)(2,1)}, u32[]{:S(2)}) copy-start(bf16[2,2,40,128]{3,2,1,0:T(8,128)(2,1)} %param.13) | copy-start | bytes 122884
  6.5 1.4 copy-start.2
  7.9 186.4 %copy-start.3 = (bf16[2,2,40,128]{3,2,1,0:T(8,128)(2,1)S(1)}, bf16[2,2,40,128]{3,2,1,0:T(8,128)(2,1)}, u32[]{:S(2)}) copy-start(bf16[2,2,40,128]{3,2,1,0:T(8,128)(2,1)} %param.12) | copy-start | bytes 122884
  12.3 4.1 %copy-start.1 = (f32[2,2,512,40,16]{2,3,4,1,0:T(8,128)S(1)}, f32[2,2,512,40,16]{2,3,4,1,0:T(8,128)}, u32[]{:S(2)}) copy-start(f32[2,2,512,40,16]{2,3,4,1,0:T(8,128)} %get-tuple-element.282) | copy-start | bytes 15728644 | tf_op jit(solution)/shard_map/while
  24.0 4.1 %copy-start.1 = (f32[2,2,512,40,16]{2,3,4,1,0:T(8,128)S(1)}, f32[2,2,512,40,16]{2,3,4,1,0:T(8,128)}, u32[]{:S(2)}) copy-start(f32[2,2,512,40,16]{2,3,4,1,0:T(8,128)} %get-tuple-element.282) | copy-start | bytes 15728644 | tf_op jit(solution)/shard_map/while
  35.6 4.1 %copy-start.1 = (f32[2,2,512,40,16]{2,3,4,1,0:T(8,128)S(1)}, f32[2,2,512,40,16]{2,3,4,1,0:T(8,128)}, u32[]{:S(2)}) copy-start(f32[2,2,512,40,16]{2,3,4,1,0:T(8,128)} %get-tuple-element.282) | copy-start | bytes 15728644 | tf_op jit(solution)/shard_map/while
  47.3 4.1 %copy-start.1 = (f32[2,2,512,40,16]{2,3,4,1,0:T(8,128)S(1)}, f32[2,2,512,40,16]{2,3,4,1,0:T(8,128)}, u32[]{:S(2)}) copy-start(f32[2,2,512,40,16]{2,3,4,1,0:T(8,128)} %get-tuple-element.282) | copy-start | bytes 15728644 | tf_op jit(solution)/shard_map/while
  58.9 4.1 %copy-start.1 = (f32[2,2,512,40,16]{2,3,4,1,0:T(8,128)S(1)}, f32[2,2,512,40,16]{2,3,4,1,0:T(8,128)}, u32[]{:S(2)}) copy-start(f32[2,2,512,40,16]{2,3,4,1,0:T(8,128)} %get-tuple-element.282) | copy-start | bytes 15728644 | tf_op jit(solution)/shard_map/while
  70.5 4.1 %copy-start.1 = (f32[2,2,512,40,16]{2,3,4,1,0:T(8,128)S(1)}, f32[2,2,512,40,16]{2,3,4,1,0:T(8,128)}, u32[]{:S(2)}) copy-start(f32[2,2,512,40,16]{2,3,4,1,0:T(8,128)} %get-tuple-element.282) | copy-start | bytes 15728644 | tf_op jit(solution)/shard_map/while
  82.2 4.1 %copy-start.1 = (f32[2,2,512,40,16]{2,3,4,1,0:T(8,128)S(1)}, f32[2,2,512,40,16]{2,3,4,1,0:T(8,128)}, u32[]{:S(2)}) copy-start(f32[2,2,512,40,16]{2,3,4,1,0:T(8,128)} %get-tuple-element.282) | copy-start | bytes 15728644 | tf_op jit(solution)/shard_map/while
  93.8 4.1 %copy-start.1 = (f32[2,2,512,40,16]{2,3,4,1,0:T(8,128)S(1)}, f32[2,2,512,40,16]{2,3,4,1,0:T(8,128)}, u32[]{:S(2)}) copy-start(f32[2,2,512,40,16]{2,3,4,1,0:T(8,128)} %get-tuple-element.282) | copy-start | bytes 15728644 | tf_op jit(solution)/shard_map/while
  105.4 4.1 %copy-start.1 = (f32[2,2,512,40,16]{2,3,4,1,0:T(8,128)S(1)}, f32[2,2,512,40,16]{2,3,4,1,0:T(8,128)}, u32[]{:S(2)}) copy-start(f32[2,2,512,40,16]{2,3,4,1,0:T(8,128)} %get-tuple-element.282) | copy-start | bytes 15728644 | tf_op jit(solution)/shard_map/while
  117.1 4.1 %copy-start.1 = (f32[2,2,512,40,16]{2,3,4,1,0:T(8,128)S(1)}, f32[2,2,512,40,16]{2,3,4,1,0:T(8,128)}, u32[]{:S(2)}) copy-start(f32[2,2,512,40,16]{2,3,4,1,0:T(8,128)} %get-tuple-element.282) | copy-start | bytes 15728644 | tf_op jit(solution)/shard_map/while
  128.7 4.1 %copy-start.1 = (f32[2,2,512,40,16]{2,3,4,1,0:T(8,128)S(1)}, f32[2,2,512,40,16]{2,3,4,1,0:T(8,128)}, u32[]{:S(2)}) copy-start(f32[2,2,512,40,16]{2,3,4,1,0:T(8,128)} %get-tuple-element.282) | copy-start | bytes 15728644 | tf_op jit(solution)/shard_map/while
  140.4 4.1 %copy-start.1 = (f32[2,2,512,40,16]{2,3,4,1,0:T(8,128)S(1)}, f32[2,2,512,40,16]{2,3,4,1,0:T(8,128)}, u32[]{:S(2)}) copy-start(f32[2,2,512,40,16]{2,3,4,1,0:T(8,128)} %get-tuple-element.282) | copy-start | bytes 15728644 | tf_op jit(solution)/shard_map/while
  152.0 4.1 %copy-start.1 = (f32[2,2,512,40,16]{2,3,4,1,0:T(8,128)S(1)}, f32[2,2,512,40,16]{2,3,4,1,0:T(8,128)}, u32[]{:S(2)}) copy-start(f32[2,2,512,40,16]{2,3,4,1,0:T(8,128)} %get-tuple-element.282) | copy-start | bytes 15728644 | tf_op jit(solution)/shard_map/while
  163.6 4.1 %copy-start.1 = (f32[2,2,512,40,16]{2,3,4,1,0:T(8,128)S(1)}, f32[2,2,512,40,16]{2,3,4,1,0:T(8,128)}, u32[]{:S(2)}) copy-start(f32[2,2,512,40,16]{2,3,4,1,0:T(8,128)} %get-tuple-element.282) | copy-start | bytes 15728644 | tf_op jit(solution)/shard_map/while
  175.3 4.1 %copy-start.1 = (f32[2,2,512,40,16]{2,3,4,1,0:T(8,128)S(1)}, f32[2,2,512,40,16]{2,3,4,1,0:T(8,128)}, u32[]{:S(2)}) copy-start(f32[2,2,512,40,16]{2,3,4,1,0:T(8,128)} %get-tuple-element.282) | copy-start | bytes 15728644 | tf_op jit(solution)/shard_map/while
  186.9 4.1 %copy-start.1 = (f32[2,2,512,40,16]{2,3,4,1,0:T(8,128)S(1)}, f32[2,2,512,40,16]{2,3,4,1,0:T(8,128)}, u32[]{:S(2)}) copy-start(f32[2,2,512,40,16]{2,3,4,1,0:T(8,128)} %get-tuple-element.282) | copy-start | bytes 15728644 | tf_op jit(solution)/shard_map/while
  197.7 11.8 %all-to-all-start.2 = ((f32[80,8,4]{0,2,1:T(4,128)}), f32[80,8,4]{0,2,1:T(4,128)S(1)}, u32[]{:S(2)}, u32[]{:S(2)}) async-start(f32[80,8,4]{0,2,1:T(4,128)} %reshape_reshape_broadcast_in_dim_reshape.7), calls=%async_computation.2 | async-start | bytes 32768 | tf_op jit(solution)/shard_map/all_to_all | solution.py:80
  209.4 8.7 %all-to-all-start.1 = ((f32[80,8,4]{0,2,1:T(4,128)}), f32[80,8,4]{0,2,1:T(4,128)S(1)}, u32[]{:S(2)}, u32[]{:S(2)}) async-start(f32[80,8,4]{0,2,1:T(4,128)} %reshape_reshape_broadcast_in_dim_reshape.6), calls=%async_computation.1 | async-start | bytes 32768 | tf_op jit(solution)/shard_map/all_to_all | solution.py:79
  218.1 32.7 %all-to-all-start = ((f32[80,8,512]{2,0,1:T(8,128)}), f32[80,8,512]{2,0,1:T(8,128)S(1)}, u32[]{:S(2)}, u32[]{:S(2)}) async-start(f32[80,8,512]{2,0,1:T(8,128)} %copy.30), calls=%async_computation | async-start | bytes 2621440 | tf_op jit(solution)/shard_map/all_to_all | solution.py:78
  221.7 95.2 %reduce-scatter.2.cloned.1.call-start = ((), (), s32[]{:S(2)}) async-start(), calls=%async_computation.4 | async-start | bytes 819200 | tf_op jit(solution)/shard_map/reduce_scatter | solution.py:94
Sparse Core Ops, SparseCore 0:
  287.9 29.0 reduce-scatter.1
where the time goes:
time: 327 us; the launch traced here: 325 us
  matrix products  132 us (40%)
  other arithmetic  63.4 us (19%)
  waiting for transfers between devices  60.8 us (19%)
  blocking collectives  26.8 us (8%)
  local copies, waits for them, and re-layouts  14.5 us (4%)
  between operations  13.6 us (4%)
  starting transfers between devices  13.3 us (4%)
    dot_general x16, matrix products, cache_block(): jnp.einsum('bjkgd,bktd->bkjgt', queries, key_block, preferred_element_typ...  68.4 us
    reduce_sum x17, other arithmetic, absorb(): run_sum = run_sum * factor + jnp.sum(weights, axis=-1)  59.7 us
    dot_general x17, matrix products, absorb(): jnp.einsum('bkjgt,bktd->bkjgd', weights, values.astype(jnp.float32), pref...  52.2 us
    reduce_scatter x1, waiting for transfers between devices, per_device(): lax.psum_scatter(partial_value, 'head', scatter_dimension=1, tiled=True)  29.2 us
    all_gather x1, blocking collectives, per_device(): lax.all_gather(attention, 'kv', axis=1, tiled=True)  26.8 us
    all_to_all x1, waiting for transfers between devices, per_device(): lax.all_to_all(sent_mix, 'kv', split_axis=1, concat_axis=1, tiled=True)  25.3 us
    dot_general x1, matrix products, per_device(): jnp.dot(lax.all_gather(attention, 'kv', axis=1, tiled=True), out_weight,...  9.64 us
  transfers between devices with their start and end apart: 4, of which 4 were waited for; matrix products, arithmetic and copies ran while one was open for 3% of the time, Pallas kernels for 0%

commit v1 on v0

--- a/solution.py
+++ b/solution.py
@@ -1,14 +1,384 @@
+import functools
 import math
 
 import jax
 import jax.numpy as jnp
 from jax import lax
+from jax.experimental import pallas as pl
+from jax.experimental.pallas import tpu as pltpu
 from jax.sharding import PartitionSpec as P
 
 masked_score = -1e30
+MESH = pl.DeviceIdType.MESH
+f32 = jnp.float32
+bf16 = jnp.bfloat16
+
+
+def attend_kernel(chunk, kv_count, lengths_ref, q_ref, k_ref, v_ref, dk_ref, dv_ref, acc_out, stat_out, acc, top):
+    draft, group, width = q_ref.shape[1], q_ref.shape[2], q_ref.shape[3]
+    rows = draft * group
+    span = k_ref.shape[2]
+    request = pl.program_id(1)
+    step = pl.program_id(2)
+    steps = pl.num_programs(2)
+    kv_index = lax.axis_index("kv")
+    scale = math.log2(math.e) / math.sqrt(width)
+    queries = q_ref[...].reshape(rows, width)
+    chunks = rows // chunk
+    contract_last = (((1,), (1,)), ((), ()))
+
+    def scores_of(index, keys):
+        part = queries[index * chunk : (index + 1) * chunk]
+        return lax.dot_general(part, keys, contract_last, preferred_element_type=f32)
+
+    def with_ones(values):
+        return jnp.concatenate([values, jnp.ones(values.shape, bf16)], axis=1)
+
+    @pl.when(step == 0)
+    def _():
+        keys = dk_ref[0, 0]
+        values = with_ones(dv_ref[0, 0])
+        for index in range(chunks):
+            scores = scores_of(index, keys)
+            owner = (lax.broadcasted_iota(jnp.int32, scores.shape, 0) + index * chunk) // group
+            place = lax.broadcasted_iota(jnp.int32, scores.shape, 1)
+            live = jnp.logical_and(place <= owner, kv_index == kv_count - 1)
+            scores = jnp.where(live, scores * scale, masked_score)
+            peak = jnp.max(scores, axis=1, keepdims=True)
+            weights = jnp.exp2(scores - peak).astype(bf16)
+            here = pl.ds(index * chunk, chunk)
+            top[here, :] = jnp.broadcast_to(peak, (chunk, width))
+            acc[here, :] = jnp.dot(weights, values, preferred_element_type=f32)
+
+    first = kv_index * (span * steps) + step * span
+    length = lengths_ref[request]
+
+    def block(masked):
+        keys = k_ref[0, 0]
+        values = with_ones(v_ref[0, 0])
+        if masked:
+            live = first + lax.broadcasted_iota(jnp.int32, (1, span), 1) < length
+        ahead = scores_of(0, keys)
+        for index in range(chunks):
+            scores = ahead
+            if index + 1 < chunks:
+                ahead = scores_of(index + 1, keys)
+            if masked:
+                scores = jnp.where(live, scores, masked_score)
+            here = pl.ds(index * chunk, chunk)
+            old = top[here, :]
+            new = jnp.maximum(old, jnp.max(scores, axis=1, keepdims=True) * scale)
+            weights = jnp.exp2(scores * scale - new[:, :1]).astype(bf16)
+            factor = jnp.exp2(old - new)
+            top[here, :] = new
+            acc[here, :] = acc[here, :] * jnp.concatenate([factor, factor], axis=1) + jnp.dot(
+                weights, values, preferred_element_type=f32
+            )
+
+    whole = first + span <= length
+
+    @pl.when(whole)
+    def _():
+        block(False)
+
+    @pl.when(jnp.logical_and(jnp.logical_not(whole), first < length))
+    def _():
+        block(True)
+
+    @pl.when(step == steps - 1)
+    def _():
+        acc_out[0] = acc[:, :width].astype(bf16)
+        share = rows // kv_count
+        diagonal = lax.broadcasted_iota(jnp.int32, (share, width), 0) == lax.broadcasted_iota(
+            jnp.int32, (share, width), 1
+        )
+        line = lax.broadcasted_iota(jnp.int32, (8, width), 0)
+        for dest in range(kv_count):
+            here = pl.ds(dest * share, share)
+            peaks = jnp.sum(jnp.where(diagonal, top[here, :], 0.0), axis=0, keepdims=True)
+            sums = jnp.sum(jnp.where(diagonal, acc[here, width:], 0.0), axis=0, keepdims=True)
+            stat_out[0, dest] = jnp.where(line == 0, peaks, jnp.where(line == 1, sums, 0.0))
+
+
+def attend(query, key_cache, value_cache, draft_keys, draft_values, lengths, kv_count):
+    batch, draft, qheads, width = query.shape
+    kv_heads, local_span = key_cache.shape[1], key_cache.shape[2]
+    group = qheads // kv_heads
+    rows = draft * group
+    span = min(2048, local_span)
+    chunk = 128 if rows % 128 == 0 else rows
+    units = batch * kv_heads
+    cache_spec = pl.BlockSpec((1, 1, span, width), lambda k, b, t, *_: (b, k, t, 0))
+    draft_spec = pl.BlockSpec((1, 1, draft, width), lambda k, b, t, *_: (b, k, 0, 0))
+    return pl.pallas_call(
+        functools.partial(attend_kernel, chunk, kv_count),
+        grid_spec=pltpu.PrefetchScalarGridSpec(
+            num_scalar_prefetch=1,
+            grid=(kv_heads, batch, local_span // span),
+            in_specs=[
+                pl.BlockSpec((1, draft, group, width), lambda k, b, t, *_: (b, 0, k, 0)),
+                cache_spec,
+                cache_spec,
+                draft_spec,
+                draft_spec,
+            ],
+            out_specs=[
+                pl.BlockSpec((1, rows, width), lambda k, b, t, *_: (k * batch + b, 0, 0)),
+                pl.BlockSpec((1, kv_count, 8, width), lambda k, b, t, *_: (k * batch + b, 0, 0, 0)),
+            ],
+            scratch_shapes=[pltpu.VMEM((rows, 2 * width), f32), pltpu.VMEM((rows, width), f32)],
+        ),
+        out_shape=[
+            jax.ShapeDtypeStruct((units, rows, width), bf16),
+            jax.ShapeDtypeStruct((units, kv_count, 8, width), f32),
+        ],
+        compiler_params=pltpu.CompilerParams(vmem_limit_bytes=48 * 1024 * 1024),
+        cost_estimate=pl.CostEstimate(
+            flops=4 * units * rows * local_span * width,
+            bytes_accessed=4 * units * local_span * width,
+            transcendentals=units * rows * local_span,
+        ),
+    )(lengths, query, key_cache, value_cache, draft_keys, draft_values)
+
+
+def finish_kernel(
+    kv_count, head_count, batch, group,
+    acc_ref, stat_ref, w_ref, out_ref,
+    weight, got_acc, got_stat, gathered, wide, lhs, sent, got_part,
+    w_sem, acc_send, acc_recv, stat_send, stat_recv, near_send, far_send, gather_recv, part_send, part_recv,
+):
+    units, rows, width = acc_ref.shape
+    share = rows // kv_count
+    draft = rows // group
+    columns = weight.shape[2]
+    me = lax.axis_index("kv")
+    head = lax.axis_index("head")
+
+    def load(h):
+        return pltpu.make_async_copy(w_ref.at[:, pl.ds(h * columns, columns)], weight.at[h], w_sem.at[h])
+
+    for h in range(head_count):
+        load(h).start()
+
+    barrier = pltpu.get_barrier_semaphore()
+    for ahead in range(1, kv_count):
+        pl.semaphore_signal(barrier, inc=1, device_id={"kv": lax.rem(me + ahead, kv_count)}, device_id_type=MESH)
+    for ahead in range(1, head_count):
+        pl.semaphore_signal(barrier, inc=1, device_id={"head": lax.rem(head + ahead, head_count)}, device_id_type=MESH)
+    pl.semaphore_wait(barrier, kv_count + head_count - 2)
+
+    def acc_copy(dest, source):
+        return pltpu.make_async_remote_copy(
+            src_ref=acc_ref.at[:, pl.ds(pl.multiple_of(dest * share, 16), share), :],
+            dst_ref=got_acc.at[source],
+            send_sem=acc_send.at[dest],
+            recv_sem=acc_recv.at[source],
+            device_id={"kv": dest},
+            device_id_type=MESH,
+        )
+
+    def stat_copy(dest, source):
+        return pltpu.make_async_remote_copy(
+            src_ref=stat_ref.at[:, dest],
+            dst_ref=got_stat.at[source],
+            send_sem=stat_send.at[dest],
+            recv_sem=stat_recv.at[source],
+            device_id={"kv": dest},
+            device_id_type=MESH,
+        )
+
+    for ahead in range(1, kv_count):
+        dest = lax.rem(me + ahead, kv_count)
+        stat_copy(dest, me).start()
+        acc_copy(dest, me).start()
+    got_stat[me] = stat_ref[:, me]
+    got_acc[me] = acc_ref[:, pl.ds(pl.multiple_of(me * share, 16), share), :]
+    for ahead in range(1, kv_count):
+        other = lax.rem(me + ahead, kv_count)
+        stat_copy(other, other).wait_recv()
+        acc_copy(other, other).wait_recv()
+
+    diagonal = lax.broadcasted_iota(jnp.int32, (share, width), 0) == lax.broadcasted_iota(
+        jnp.int32, (share, width), 1
+    )
+    for unit in range(units):
+        peaks = [got_stat[source, unit][0:1, :] for source in range(kv_count)]
+        peak = functools.reduce(jnp.maximum, peaks)
+        factors = [jnp.exp2(value - peak) for value in peaks]
+        total = sum(got_stat[source, unit][1:2, :] * factors[source] for source in range(kv_count))
+        merged = jnp.zeros((share, width), f32)
+        for source in range(kv_count):
+            portion = jnp.broadcast_to(factors[source] / total, (share, width))
+            column = jnp.sum(jnp.where(diagonal, portion, 0.0), axis=1, keepdims=True)
+            merged = merged + got_acc[source, unit].astype(f32) * column
+        gathered[me, unit] = merged.astype(bf16)
+
+    partner = me + 1 - 2 * lax.rem(me, 2)
+    half = kv_count // 2
+
+    def near_copy(block):
+        return pltpu.make_async_remote_copy(
+            src_ref=gathered.at[block],
+            dst_ref=gathered.at[block],
+            send_sem=near_send.at[block],
+            recv_sem=gather_recv.at[block],
+            device_id={"kv": partner},
+            device_id_type=MESH,
+        )
+
+    def far_copy(dest, block):
+        return pltpu.make_async_remote_copy(
+            src_ref=gathered.at[block],
+            dst_ref=gathered.at[block],
+            send_sem=far_send.at[dest],
+            recv_sem=gather_recv.at[block],
+            device_id={"kv": dest},
+            device_id_type=MESH,
+        )
+
+    for ahead in range(1, half):
+        far_copy(lax.rem(me + 2 * ahead, kv_count), me).start()
+    near_copy(me).start()
+
+    def widen(block):
+        for unit in range(units):
+            wide[unit, pl.ds(pl.multiple_of(block * share, 16), share), :] = gathered[block, unit].astype(f32)
+
+    widen(me)
+    for ahead in range(1, half):
+        block = lax.rem(me + kv_count - 2 * ahead, kv_count)
+        far_copy(block, block).wait_recv()
+        near_copy(block).start()
+        widen(block)
+    for ahead in range(half):
+        block = lax.rem(partner + kv_count - 2 * ahead, kv_count)
+        near_copy(block).wait_recv()
+        widen(block)
+
+    for head_group in range(units // batch):
+        for member in range(group):
+            pieces = [
+                wide[head_group * batch + request, pl.ds(member, draft, stride=group), :]
+                for request in range(batch)
+            ]
+            place = (head_group * group + member) * width
+            lhs[:, place : place + width] = jnp.concatenate(pieces, axis=0).astype(bf16)
+
+    def part_copy(dest, source):
+        return pltpu.make_async_remote_copy(
+            src_ref=sent.at[dest],
+            dst_ref=got_part.at[source],
+            send_sem=part_send.at[dest],
+            recv_sem=part_recv.at[source],
+            device_id={"head": dest},
+            device_id_type=MESH,
+        )
+
+    for h in range(head_count):
+        load(h).wait()
+
+    @pl.loop(1, head_count)
+    def _(ahead):
+        dest = lax.rem(head + ahead, head_count)
+        sent[dest] = jnp.dot(lhs[...], weight[dest], preferred_element_type=f32).astype(bf16)
+        part_copy(dest, head).start()
+
+    result = jnp.dot(lhs[...], weight[head], preferred_element_type=f32)
+    for ahead in range(1, head_count):
+        source = lax.rem(head + ahead, head_count)
+        part_copy(source, source).wait_recv()
+        result = result + got_part[source].astype(f32)
+    for request in range(batch):
+        out_ref[request] = result[request * draft : (request + 1) * draft].astype(bf16)
+
+    for ahead in range(1, kv_count):
+        dest = lax.rem(me + ahead, kv_count)
+        stat_copy(dest, me).wait_send()
+        acc_copy(dest, me).wait_send()
+    for ahead in range(1, half):
+        far_copy(lax.rem(me + 2 * ahead, kv_count), me).wait_send()
+    for ahead in range(half):
+        near_copy(lax.rem(me + 2 * ahead, kv_count)).wait_send()
+    for ahead in range(1, head_count):
+        part_copy(lax.rem(head + ahead, head_count), head).wait_send()
+
+
+def finish(acc, stats, out_weight, kv_count, head_count, batch, group):
+    units, rows, width = acc.shape
+    share = rows // kv_count
+    draft = rows // group
+    features, out_width = out_weight.shape
+    columns = out_width // head_count
+    tokens = batch * draft
+    dma = pltpu.SemaphoreType.DMA
+    return pl.pallas_call(
+        functools.partial(finish_kernel, kv_count, head_count, batch, group),
+        out_shape=jax.ShapeDtypeStruct((batch, draft, columns), bf16),
+        in_specs=[
+            pl.BlockSpec(memory_space=pltpu.VMEM),
+            pl.BlockSpec(memory_space=pltpu.VMEM),
+            pl.BlockSpec(memory_space=pl.ANY),
+        ],
+        out_specs=pl.BlockSpec(memory_space=pltpu.VMEM),
+        scratch_shapes=[
+            pltpu.VMEM((head_count, features, columns), bf16),
+            pltpu.VMEM((kv_count, units, share, width), bf16),
+            pltpu.VMEM((kv_count, units, 8, width), f32),
+            pltpu.VMEM((kv_count, units, share, width), bf16),
+            pltpu.VMEM((units, rows, width), f32),
+            pltpu.VMEM((tokens, features), bf16),
+            pltpu.VMEM((head_count, tokens, columns), bf16),
+            pltpu.VMEM((head_count, tokens, columns), bf16),
+            dma((head_count,)),
+            dma((kv_count,)),
+            dma((kv_count,)),
+            dma((kv_count,)),
+            dma((kv_count,)),
+            dma((kv_count,)),
+            dma((kv_count,)),
+            dma((kv_count,)),
+            dma((head_count,)),
+            dma((head_count,)),
+        ],
+        compiler_params=pltpu.CompilerParams(
+            collective_id=0, has_side_effects=True, vmem_limit_bytes=48 * 1024 * 1024
+        ),
+        cost_estimate=pl.CostEstimate(
+            flops=2 * tokens * features * out_width,
+            bytes_accessed=2 * features * out_width,
+            transcendentals=0,
+        ),
+    )(acc, stats, out_weight)
+
+
+def fast_per_device(query, key_cache, value_cache, draft_keys, draft_values, lengths, out_weight):
+    batch, draft, qheads, width = query.shape
+    group = qheads // key_cache.shape[1]
+    kv_count, head_count = lax.axis_size("kv"), lax.axis_size("head")
+    acc, stats = attend(query, key_cache, value_cache, draft_keys, draft_values, lengths, kv_count)
+    return finish(acc, stats, out_weight, kv_count, head_count, batch, group)
+
+
+def fits(query, key_cache, out_weight, kv_count, head_count):
+    batch, draft, qheads, width = query.shape
+    rows = draft * (qheads // key_cache.shape[1])
+    share = rows // kv_count
+    return (
+        kv_count % 2 == 0
+        and rows % kv_count == 0
+        and share % 16 == 0
+        and share <= width
+        and width == 128
+        and draft % 8 == 0
+        and out_weight.shape[1] % (128 * head_count) == 0
+    )
 
 
 def per_device(query, key_cache, value_cache, draft_keys, draft_values, lengths, out_weight):
+    if fits(query, key_cache, out_weight, lax.axis_size("kv"), lax.axis_size("head")):
+        return fast_per_device(
+            query, key_cache, value_cache, draft_keys, draft_values, lengths, out_weight
+        )
     batch, draft, qheads, head_width = query.shape
     kv_heads = key_cache.shape[1]
     local_span = key_cache.shape[2]

time: 327 us -> 88.7 us (0.27)
  matrix products: 132 us -> 0 us
  Pallas kernels: 0 us -> 84.4 us
  other arithmetic: 63.4 us -> 0 us
  waiting for transfers between devices: 60.8 us -> 0 us
  blocking collectives: 26.8 us -> 0 us
  between operations: 13.6 us -> 0.02 us
  starting transfers between devices: 13.3 us -> 0 us
  local copies, waits for them, and re-layouts: 14.5 us -> 3.94 us
    dot_general x35 -> x0, matrix products: 132 us -> none  [the longest x16 68.4 us: cache_block(): jnp.einsum('bjkgd,bktd->bkjgt', queries, key_block, preferred_element_typ...]
    pallas_call x0 -> x2, Pallas kernels: none -> 84.4 us  [the longest x1 46.5 us: finish(): pl.pallas_call(functools.partial(finish_kernel, kv_count, head_count, bat...]
    reduce_sum x19 -> x0, other arithmetic: 60 us -> none  [the longest x17 59.7 us: absorb(): run_sum = run_sum * factor + jnp.sum(weights, axis=-1)]
    all_to_all x3 -> x0, waiting for transfers between devices: 31.6 us -> none  [the longest x1 25.3 us: per_device(): lax.all_to_all(sent_mix, 'kv', split_axis=1, concat_axis=1, tiled=True)]
    reduce_scatter x1 -> x0, waiting for transfers between devices: 29.2 us -> none  [per_device(): lax.psum_scatter(partial_value, 'head', scatter_dimension=1, tiled=True)]
    all_gather x1 -> x0, blocking collectives: 26.8 us -> none  [per_device(): lax.all_gather(attention, 'kv', axis=1, tiled=True)]
    all_to_all x3 -> x0, starting transfers between devices: 13.3 us -> none  [the longest x1 6.34 us: per_device(): lax.all_to_all(sent_sum, 'kv', split_axis=1, concat_axis=1, tiled=True)]
    while x50 -> x0, local copies, waits for them, and re-layouts: 5.5 us -> none
  transfers between devices with their start and end apart: 4 -> 0, of which waited for: 4 -> 0; matrix products, arithmetic and copies ran while one was open for 3% -> 0% of each run, Pallas kernels for 0% -> 0%
where the time goes in v1:
time: 88.7 us; the launch traced here: 88.4 us
  Pallas kernels  84.4 us (95%)
  local copies, waits for them, and re-layouts  3.94 us (4%)
    pallas_call x1, Pallas kernels, finish(): pl.pallas_call(functools.partial(finish_kernel, kv_count, head_count, bat...  46.5 us
    pallas_call x1, Pallas kernels, attend(): pl.pallas_call(functools.partial(attend_kernel, chunk, kv_count), grid_sp...  38 us
    unnamed x9, local copies, waits for them, and re-layouts  3.94 us

profile of v1, /device:TPU:1, one launch (start us, length us, event | category | flops | bytes accessed | tf_op | source)
XLA Modules:
  0.0 88.4 jit_solution(16788777745455944719)
XLA Ops:
  0.0 0.0 copy-start
  0.0 1.1 %copy-done = bf16[2,40,32,128]{3,2,1,0:T(8,128)(2,1)S(1)} copy-done((bf16[2,40,32,128]{3,2,1,0:T(8,128)(2,1)S(1)}, bf16[2,40,32,128]{3,2,1,0:T(8,128)(2,1)}, u32[]{:S(2)}) %copy-start) | copy-done | bytes 655384
  1.1 0.0 copy-start.1
  1.1 0.8 copy-done.1
  1.9 0.0 copy-start.2
  1.9 0.8 copy-done.2
  2.6 0.0 copy-start.3
  2.6 0.7 copy-done.3
  3.3 38.0 %shard_map.73 = (bf16[4,640,128]{2,1,0:T(8,128)(2,1)S(1)}, f32[4,8,8,128]{3,2,1,0:T(8,128)S(1)}) custom-call(s32[2]{0:T(128)S(1)} %copy-done.3, bf16[2,40,32,128]{3,2,1,0:T(8,128)(2,1)S(1)} %copy-done, bf16[2,2,8192,128]{3,2,1,0:T(8,128)(2,1)} %k_ref.1, bf16[2,2,8192,128]{3,2,1,0:T(8,128)(2,1)} %v_ref.1, bf16[2,2,40,128]{3,2,1,0:T(8,128)(2,1)S(1)} %copy-done.1, ...), custom_call_target="tpu_custom_call" | custom-call | flops 10737418240 | bytes 16777216 | tf_op jit(solution)/shard_map/pallas_call | solution.py:113
  41.3 46.5 %shard_map.74 = bf16[2,40,512]{2,1,0:T(8,128)(2,1)S(1)} custom-call(bf16[4,640,128]{2,1,0:T(8,128)(2,1)S(1)} %get-tuple-element.7.acc_ref, f32[4,8,8,128]{3,2,1,0:T(8,128)S(1)} %get-tuple-element.8.stat_ref, bf16[4096,2048]{1,0:T(8,128)(2,1)} %w_ref.1), custom_call_target="tpu_custom_call" | custom-call | flops 1342177280 | bytes 16777216 | tf_op jit(solution)/shard_map/pallas_call | solution.py:314
  87.7 0.6 copy.9
Async XLA Ops:
  0.0 1.1 %copy-start = (bf16[2,40,32,128]{3,2,1,0:T(8,128)(2,1)S(1)}, bf16[2,40,32,128]{3,2,1,0:T(8,128)(2,1)}, u32[]{:S(2)}) copy-start(bf16[2,40,32,128]{3,2,1,0:T(8,128)(2,1)} %q_ref.1) | copy-start | bytes 1966084
  1.1 0.8 copy-start.1
  1.9 0.8 copy-start.2
  2.6 0.7 copy-start.3

commit v2 on v0

--- a/solution.py
+++ b/solution.py
@@ -1,14 +1,392 @@
+import functools
 import math
 
 import jax
 import jax.numpy as jnp
 from jax import lax
+from jax.experimental import pallas as pl
+from jax.experimental.pallas import tpu as pltpu
 from jax.sharding import PartitionSpec as P
 
 masked_score = -1e30
+MESH = pl.DeviceIdType.MESH
+f32 = jnp.float32
+bf16 = jnp.bfloat16
+contract_last = (((1,), (1,)), ((), ()))
+
+
+def layer_kernel(
+    kv_count, head_count, chunk, block, sub,
+    lengths_ref, q_hbm, k_hbm, v_hbm, dk_hbm, dv_hbm, w_hbm, out_ref,
+    query, keys, values, draft_keys, draft_values, weight, acc, top,
+    sent_acc, sent_stat, got_acc, got_stat, gathered, wide, lhs, part, sent_part, got_part,
+    small_sem, k_sem, v_sem, w_sem,
+    acc_send, acc_recv, stat_send, stat_recv, gather_send, gather_recv, part_send, part_recv,
+):
+    batch, draft, qheads, width = query.shape
+    kv_heads, local_span = k_hbm.shape[1], k_hbm.shape[2]
+    group = qheads // kv_heads
+    rows = draft * group
+    units = batch * kv_heads
+    blocks = local_span // block
+    chunks = rows // chunk
+    share = rows // kv_count
+    columns = weight.shape[2]
+    me = lax.axis_index("kv")
+    head = lax.axis_index("head")
+    scale = math.log2(math.e) / math.sqrt(width)
+
+    def split(unit):
+        return unit // batch, unit % batch
+
+    def load_keys(unit, step):
+        kv_head, request = split(unit)
+        here = pl.ds(pl.multiple_of(step * block, block), block)
+        return pltpu.make_async_copy(
+            k_hbm.at[request, kv_head, here], keys.at[unit, here], k_sem.at[unit, step]
+        )
+
+    def load_values(unit, step):
+        kv_head, request = split(unit)
+        here = pl.ds(pl.multiple_of(step * block, block), block)
+        return pltpu.make_async_copy(
+            v_hbm.at[request, kv_head, here], values.at[unit, here], v_sem.at[unit, step]
+        )
+
+    def load_weight(dest):
+        return pltpu.make_async_copy(
+            w_hbm.at[:, pl.ds(dest * columns, columns)], weight.at[dest], w_sem.at[dest]
+        )
+
+    small = [
+        pltpu.make_async_copy(source, target, small_sem.at[index])
+        for index, (source, target) in enumerate(
+            ((q_hbm, query), (dk_hbm, draft_keys), (dv_hbm, draft_values))
+        )
+    ]
+    for copy in small:
+        copy.start()
+    for unit in range(units):
+        for step in range(blocks):
+            load_keys(unit, step).start()
+            load_values(unit, step).start()
+    for dest in range(head_count):
+        load_weight(dest).start()
+
+    barrier = pltpu.get_barrier_semaphore()
+    for ahead in range(1, kv_count):
+        pl.semaphore_signal(barrier, inc=1, device_id={"kv": lax.rem(me + ahead, kv_count)}, device_id_type=MESH)
+    for ahead in range(1, head_count):
+        pl.semaphore_signal(barrier, inc=1, device_id={"head": lax.rem(head + ahead, head_count)}, device_id_type=MESH)
+    pl.semaphore_wait(barrier, kv_count + head_count - 2)
+    for copy in small:
+        copy.wait()
+
+    def acc_copy(unit, dest, source):
+        return pltpu.make_async_remote_copy(
+            src_ref=sent_acc.at[unit, pl.ds(pl.multiple_of(dest * share, 16), share)],
+            dst_ref=got_acc.at[unit, source],
+            send_sem=acc_send.at[unit, dest],
+            recv_sem=acc_recv.at[unit, source],
+            device_id={"kv": dest},
+            device_id_type=MESH,
+        )
+
+    def stat_copy(unit, dest, source):
+        return pltpu.make_async_remote_copy(
+            src_ref=sent_stat.at[unit, dest],
+            dst_ref=got_stat.at[unit, source],
+            send_sem=stat_send.at[unit, dest],
+            recv_sem=stat_recv.at[unit, source],
+            device_id={"kv": dest},
+            device_id_type=MESH,
+        )
+
+    def gather_copy(unit, dest, source):
+        return pltpu.make_async_remote_copy(
+            src_ref=gathered.at[unit, source],
+            dst_ref=gathered.at[unit, source],
+            send_sem=gather_send.at[unit, dest],
+            recv_sem=gather_recv.at[unit, source],
+            device_id={"kv": dest},
+            device_id_type=MESH,
+        )
+
+    def part_copy(dest, source):
+        return pltpu.make_async_remote_copy(
+            src_ref=sent_part.at[dest],
+            dst_ref=got_part.at[source],
+            send_sem=part_send.at[dest],
+            recv_sem=part_recv.at[source],
+            device_id={"head": dest},
+            device_id_type=MESH,
+        )
+
+    def with_ones(some):
+        return jnp.concatenate([some, jnp.ones(some.shape, bf16)], axis=1)
+
+    def unit_queries(unit):
+        kv_head, request = split(unit)
+        some = query[request, :, pl.ds(pl.multiple_of(kv_head * group, 16), group), :]
+        return some.reshape(rows, width)
+
+    def scores_of(queries, index, some):
+        mine = queries[index * chunk : (index + 1) * chunk]
+        return lax.dot_general(mine, some, contract_last, preferred_element_type=f32)
+
+    def begin(unit):
+        kv_head, request = split(unit)
+        queries = unit_queries(unit)
+        some_keys = draft_keys[request, kv_head]
+        some_values = with_ones(draft_values[request, kv_head])
+        for index in range(chunks):
+            scores = scores_of(queries, index, some_keys)
+            owner = (lax.broadcasted_iota(jnp.int32, scores.shape, 0) + index * chunk) // group
+            place = lax.broadcasted_iota(jnp.int32, scores.shape, 1)
+            live = jnp.logical_and(place <= owner, me == kv_count - 1)
+            scores = jnp.where(live, scores * scale, masked_score)
+            peak = jnp.max(scores, axis=1, keepdims=True)
+            weights = jnp.exp2(scores - peak).astype(bf16)
+            here = pl.ds(index * chunk, chunk)
+            top[here, :] = jnp.broadcast_to(peak, (chunk, width))
+            acc[here, :] = jnp.dot(weights, some_values, preferred_element_type=f32)
+
+    def attend(unit, step):
+        queries = unit_queries(unit)
+        length = lengths_ref[unit % batch]
+        items = [(piece, index) for piece in range(block // sub) for index in range(chunks)]
+
+        def scores_at(item):
+            piece, index = items[item]
+            start = pl.multiple_of(step * block + piece * sub, sub)
+            return scores_of(queries, index, keys[unit, pl.ds(start, sub), :])
+
+        ahead = scores_at(0)
+        for item, (piece, index) in enumerate(items):
+            scores = ahead
+            if item + 1 < len(items):
+                ahead = scores_at(item + 1)
+            start = pl.multiple_of(step * block + piece * sub, sub)
+            some_values = with_ones(values[unit, pl.ds(start, sub), :])
+            first = me * local_span + start
+            live = first + lax.broadcasted_iota(jnp.int32, (1, sub), 1) < length
+            scores = jnp.where(live, scores, masked_score)
+            here = pl.ds(index * chunk, chunk)
+            old = top[here, :]
+            new = jnp.maximum(old, jnp.max(scores, axis=1, keepdims=True) * scale)
+            weights = jnp.exp2(scores * scale - new[:, :1]).astype(bf16)
+            factor = jnp.exp2(old - new)
+            top[here, :] = new
+            acc[here, :] = acc[here, :] * jnp.concatenate([factor, factor], axis=1) + jnp.dot(
+                weights, some_values, preferred_element_type=f32
+            )
+
+    diagonal = lax.broadcasted_iota(jnp.int32, (share, width), 0) == lax.broadcasted_iota(
+        jnp.int32, (share, width), 1
+    )
+    line = lax.broadcasted_iota(jnp.int32, (8, width), 0)
+
+    def send(unit):
+        sent_acc[unit] = acc[:, :width].astype(bf16)
+        for dest in range(kv_count):
+            here = pl.ds(dest * share, share)
+            peaks = jnp.sum(jnp.where(diagonal, top[here, :], 0.0), axis=0, keepdims=True)
+            sums = jnp.sum(jnp.where(diagonal, acc[here, width:], 0.0), axis=0, keepdims=True)
+            sent_stat[unit, dest] = jnp.where(line == 0, peaks, jnp.where(line == 1, sums, 0.0))
+        for ahead in range(1, kv_count):
+            dest = lax.rem(me + ahead, kv_count)
+            stat_copy(unit, dest, me).start()
+            acc_copy(unit, dest, me).start()
+        got_stat[unit, me] = sent_stat[unit, me]
+        got_acc[unit, me] = sent_acc[unit, pl.ds(pl.multiple_of(me * share, 16), share)]
+
+    def merge(unit):
+        for ahead in range(1, kv_count):
+            other = lax.rem(me + ahead, kv_count)
+            stat_copy(unit, other, other).wait_recv()
+            acc_copy(unit, other, other).wait_recv()
+        peaks = [got_stat[unit, source][0:1, :] for source in range(kv_count)]
+        peak = functools.reduce(jnp.maximum, peaks)
+        factors = [jnp.exp2(value - peak) for value in peaks]
+        total = sum(got_stat[unit, source][1:2, :] * factors[source] for source in range(kv_count))
+        merged = jnp.zeros((share, width), f32)
+        for source in range(kv_count):
+            portion = jnp.broadcast_to(factors[source] / total, (share, width))
+            column = jnp.sum(jnp.where(diagonal, portion, 0.0), axis=1, keepdims=True)
+            merged = merged + got_acc[unit, source].astype(f32) * column
+        gathered[unit, me] = merged.astype(bf16)
+        for ahead in range(1, kv_count):
+            gather_copy(unit, lax.rem(me + ahead, kv_count), me).start()
+
+    def collect(unit):
+        for ahead in range(1, kv_count):
+            other = lax.rem(me + ahead, kv_count)
+            gather_copy(unit, other, other).wait_recv()
+        for source in range(kv_count):
+            wide[unit, pl.ds(source * share, share), :] = gathered[unit, source].astype(f32)
+
+    def arrange(kv_head):
+        for member in range(group):
+            pieces = [
+                wide[kv_head * batch + request, pl.ds(member, draft, stride=group), :]
+                for request in range(batch)
+            ]
+            place = (kv_head * group + member) * width
+            lhs[:, place : place + width] = jnp.concatenate(pieces, axis=0).astype(bf16)
+
+    half = (kv_heads - 1) * group * width
+
+    @pl.loop(0, units * blocks)
+    def _(index):
+        unit = index // blocks
+        step = index % blocks
+
+        @pl.when(step == 0)
+        def _():
+            begin(unit)
+
+        @pl.when(jnp.logical_and(step == blocks - 1, unit > 0))
+        def _():
+            merge(unit - 1)
+
+        load_keys(unit, step).wait()
+        load_values(unit, step).wait()
+        attend(unit, step)
+
+        @pl.when(step == blocks - 1)
+        def _():
+            send(unit)
+
+    for dest in range(head_count):
+        load_weight(dest).wait()
+    for unit in range((kv_heads - 1) * batch):
+        collect(unit)
+    for kv_head in range(kv_heads - 1):
+        arrange(kv_head)
+
+    @pl.loop(0, head_count)
+    def _(dest):
+        part[dest] = jnp.dot(lhs[:, :half], weight[dest, :half, :], preferred_element_type=f32)
+
+    merge(units - 1)
+    for unit in range((kv_heads - 1) * batch, units):
+        collect(unit)
+    arrange(kv_heads - 1)
+
+    def project(dest):
+        return part[dest] + jnp.dot(lhs[:, half:], weight[dest, half:, :], preferred_element_type=f32)
+
+    @pl.loop(1, head_count)
+    def _(ahead):
+        dest = lax.rem(head + ahead, head_count)
+        sent_part[dest] = project(dest).astype(bf16)
+        part_copy(dest, head).start()
+
+    result = project(head)
+    for ahead in range(1, head_count):
+        source = lax.rem(head + ahead, head_count)
+        part_copy(source, source).wait_recv()
+        result = result + got_part[source].astype(f32)
+    for request in range(batch):
+        out_ref[request] = result[request * draft : (request + 1) * draft].astype(bf16)
+
+    @pl.loop(0, units)
+    def _(unit):
+        for ahead in range(1, kv_count):
+            dest = lax.rem(me + ahead, kv_count)
+            stat_copy(unit, dest, me).wait_send()
+            acc_copy(unit, dest, me).wait_send()
+            gather_copy(unit, dest, me).wait_send()
+
+    for ahead in range(1, head_count):
+        part_copy(lax.rem(head + ahead, head_count), head).wait_send()
+
+
+def fast_per_device(query, key_cache, value_cache, draft_keys, draft_values, lengths, out_weight):
+    batch, draft, qheads, width = query.shape
+    kv_heads, local_span = key_cache.shape[1], key_cache.shape[2]
+    group = qheads // kv_heads
+    kv_count, head_count = lax.axis_size("kv"), lax.axis_size("head")
+    rows = draft * group
+    units = batch * kv_heads
+    share = rows // kv_count
+    features, out_width = out_weight.shape
+    columns = out_width // head_count
+    tokens = batch * draft
+    block = min(4096, local_span)
+    sub = min(2048, block)
+    blocks = local_span // block
+    chunk = 320 if rows % 320 == 0 else rows
+    dma = pltpu.SemaphoreType.DMA
+    anywhere = pl.BlockSpec(memory_space=pl.ANY)
+    return pl.pallas_call(
+        functools.partial(layer_kernel, kv_count, head_count, chunk, block, sub),
+        out_shape=jax.ShapeDtypeStruct((batch, draft, columns), bf16),
+        in_specs=[pl.BlockSpec(memory_space=pltpu.SMEM)] + [anywhere] * 6,
+        out_specs=pl.BlockSpec(memory_space=pltpu.VMEM),
+        scratch_shapes=[
+            pltpu.VMEM(query.shape, bf16),
+            pltpu.VMEM((units, local_span, width), bf16),
+            pltpu.VMEM((units, local_span, width), bf16),
+            pltpu.VMEM(draft_keys.shape, bf16),
+            pltpu.VMEM(draft_values.shape, bf16),
+            pltpu.VMEM((head_count, features, columns), bf16),
+            pltpu.VMEM((rows, 2 * width), f32),
+            pltpu.VMEM((rows, width), f32),
+            pltpu.VMEM((units, rows, width), bf16),
+            pltpu.VMEM((units, kv_count, 8, width), f32),
+            pltpu.VMEM((units, kv_count, share, width), bf16),
+            pltpu.VMEM((units, kv_count, 8, width), f32),
+            pltpu.VMEM((units, kv_count, share, width), bf16),
+            pltpu.VMEM((units, rows, width), f32),
+            pltpu.VMEM((tokens, features), bf16),
+            pltpu.VMEM((head_count, tokens, columns), f32),
+            pltpu.VMEM((head_count, tokens, columns), bf16),
+            pltpu.VMEM((head_count, tokens, columns), bf16),
+            dma((3,)),
+            dma((units, blocks)),
+            dma((units, blocks)),
+            dma((head_count,)),
+        ]
+        + [dma((units, kv_count))] * 6
+        + [dma((head_count,))] * 2,
+        compiler_params=pltpu.CompilerParams(
+            collective_id=0, has_side_effects=True, vmem_limit_bytes=60 * 1024 * 1024
+        ),
+        cost_estimate=pl.CostEstimate(
+            flops=4 * units * rows * local_span * width + 2 * tokens * features * out_width,
+            bytes_accessed=4 * units * local_span * width + 2 * features * out_width,
+            transcendentals=units * rows * local_span,
+        ),
+    )(lengths, query, key_cache, value_cache, draft_keys, draft_values, out_weight)
+
+
+def fits(query, key_cache, out_weight, kv_count, head_count):
+    batch, draft, qheads, width = query.shape
+    kv_heads, local_span = key_cache.shape[1], key_cache.shape[2]
+    group = qheads // kv_heads
+    rows = draft * group
+    share = rows // kv_count
+    held = 4 * batch * kv_heads * local_span * width + 2 * math.prod(out_weight.shape)
+    return (
+        rows % kv_count == 0
+        and share % 16 == 0
+        and share <= width
+        and width == 128
+        and draft % 8 == 0
+        and group % 16 == 0
+        and kv_heads > 1
+        and local_span % 4096 == 0
+        and held <= 36 * 1024 * 1024
+        and out_weight.shape[1] % (128 * head_count) == 0
+    )
 
 
 def per_device(query, key_cache, value_cache, draft_keys, draft_values, lengths, out_weight):
+    if fits(query, key_cache, out_weight, lax.axis_size("kv"), lax.axis_size("head")):
+        return fast_per_device(
+            query, key_cache, value_cache, draft_keys, draft_values, lengths, out_weight
+        )
     batch, draft, qheads, head_width = query.shape
     kv_heads = key_cache.shape[1]
     local_span = key_cache.shape[2]

time: 327 us -> 68.7 us (0.21)
  matrix products: 132 us -> 0 us
  Pallas kernels: 0 us -> 67 us
  other arithmetic: 63.4 us -> 0 us
  waiting for transfers between devices: 60.8 us -> 0 us
  blocking collectives: 26.8 us -> 0 us
  between operations: 13.6 us -> 0.01 us
  starting transfers between devices: 13.3 us -> 0 us
  local copies, waits for them, and re-layouts: 14.5 us -> 1.53 us
    dot_general x35 -> x0, matrix products: 132 us -> none  [the longest x16 68.4 us: cache_block(): jnp.einsum('bjkgd,bktd->bkjgt', queries, key_block, preferred_element_typ...]
    pallas_call x0 -> x1, Pallas kernels: none -> 67 us  [fast_per_device(): pl.pallas_call(functools.partial(layer_kernel, kv_count, head_count, chun...]
    reduce_sum x19 -> x0, other arithmetic: 60 us -> none  [the longest x17 59.7 us: absorb(): run_sum = run_sum * factor + jnp.sum(weights, axis=-1)]
    all_to_all x3 -> x0, waiting for transfers between devices: 31.6 us -> none  [the longest x1 25.3 us: per_device(): lax.all_to_all(sent_mix, 'kv', split_axis=1, concat_axis=1, tiled=True)]
    reduce_scatter x1 -> x0, waiting for transfers between devices: 29.2 us -> none  [per_device(): lax.psum_scatter(partial_value, 'head', scatter_dimension=1, tiled=True)]
    all_gather x1 -> x0, blocking collectives: 26.8 us -> none  [per_device(): lax.all_gather(attention, 'kv', axis=1, tiled=True)]
    all_to_all x3 -> x0, starting transfers between devices: 13.3 us -> none  [the longest x1 6.34 us: per_device(): lax.all_to_all(sent_sum, 'kv', split_axis=1, concat_axis=1, tiled=True)]
    while x50 -> x0, local copies, waits for them, and re-layouts: 5.5 us -> none
  transfers between devices with their start and end apart: 4 -> 0, of which waited for: 4 -> 0; matrix products, arithmetic and copies ran while one was open for 3% -> 0% of each run, Pallas kernels for 0% -> 0%
where the time goes in v2:
time: 68.7 us; the launch traced here: 68.5 us
  Pallas kernels  67 us (98%)
  local copies, waits for them, and re-layouts  1.53 us (2%)
    pallas_call x1, Pallas kernels, fast_per_device(): pl.pallas_call(functools.partial(layer_kernel, kv_count, head_count, chun...  67 us
    unnamed x1, local copies, waits for them, and re-layouts  1.53 us

profile of v2, /device:TPU:1, one launch (start us, length us, event | category | flops | bytes accessed | tf_op | source)
XLA Modules:
  0.0 68.5 jit_solution(15320097004842736956)
XLA Ops:
  0.0 67.0 %shard_map.73 = bf16[2,40,512]{2,1,0:T(8,128)(2,1)} custom-call(s32[2]{0:T(128)} %lengths_ref.1, bf16[2,40,32,128]{3,2,1,0:T(8,128)(2,1)} %q_hbm.1, bf16[2,2,8192,128]{3,2,1,0:T(8,128)(2,1)} %k_hbm.1, bf16[2,2,8192,128]{3,2,1,0:T(8,128)(2,1)} %v_hbm.1, bf16[2,2,40,128]{3,2,1,0:T(8,128)(2,1)} %dk_hbm.1, bf16[2,2,40,128]{3,2,1,0:T(8,128)(2,1)} %dv_hbm.1, ...), custom_call_target="tpu_custom_call" | custom-call | flops 12079595520 | bytes 33554432 | tf_op jit(solution)/shard_map/pallas_call | solution.py:322
  67.0 1.5 %copy.9 = bf16[2,40,512]{2,1,0:T(8,128)(2,1)} copy(bf16[2,40,512]{2,1,0:T(8,128)(2,1)} %shard_map.73) | data formatting | bytes 163840

commit v3 on v2

--- a/solution.py
+++ b/solution.py
@@ -16,9 +16,9 @@
 
 
 def layer_kernel(
-    kv_count, head_count, chunk, block, sub,
+    kv_count, head_count, chunk, block, sub, tile_width,
     lengths_ref, q_hbm, k_hbm, v_hbm, dk_hbm, dv_hbm, w_hbm, out_ref,
-    query, keys, values, draft_keys, draft_values, weight, acc, top,
+    query, keys, values, draft_keys, draft_values, weight, acc, top, next_scores, next_highest,
     sent_acc, sent_stat, got_acc, got_stat, gathered, wide, lhs, part, sent_part, got_part,
     small_sem, k_sem, v_sem, w_sem,
     acc_send, acc_recv, stat_send, stat_recv, gather_send, gather_recv, part_send, part_recv,
@@ -151,35 +151,63 @@
             top[here, :] = jnp.broadcast_to(peak, (chunk, width))
             acc[here, :] = jnp.dot(weights, some_values, preferred_element_type=f32)
 
-    def attend(unit, step):
-        queries = unit_queries(unit)
-        length = lengths_ref[unit % batch]
+    def score_tile(unit, step, piece, index, tile):
+        start = pl.multiple_of(step * block + piece * sub + tile * tile_width, tile_width)
+        scores = scores_of(unit_queries(unit), index, keys[unit, pl.ds(start, tile_width), :])
+        first = me * local_span + start
+        live = first + lax.broadcasted_iota(jnp.int32, (1, tile_width), 1) < lengths_ref[unit % batch]
+        return jnp.where(live, scores, masked_score)
+
+    def lane_max(known, scores):
+        for lane in range(0, tile_width, width):
+            here = scores[:, lane : lane + width]
+            known = here if known is None else jnp.maximum(known, here)
+        return known
+
+    tiles = sub // tile_width
+
+    def prime():
+        highest = None
+        for tile in range(tiles):
+            scores = score_tile(0, 0, 0, 0, tile)
+            highest = lane_max(highest, scores)
+            next_scores[:, tile * tile_width : (tile + 1) * tile_width] = scores
+        next_highest[...] = highest
+
+    def attend(unit, step, next_unit, next_step):
         items = [(piece, index) for piece in range(block // sub) for index in range(chunks)]
-
-        def scores_at(item):
-            piece, index = items[item]
-            start = pl.multiple_of(step * block + piece * sub, sub)
-            return scores_of(queries, index, keys[unit, pl.ds(start, sub), :])
-
-        ahead = scores_at(0)
+        current = [next_scores[:, tile * tile_width : (tile + 1) * tile_width] for tile in range(tiles)]
+        highest = next_highest[...]
         for item, (piece, index) in enumerate(items):
-            scores = ahead
-            if item + 1 < len(items):
-                ahead = scores_at(item + 1)
-            start = pl.multiple_of(step * block + piece * sub, sub)
-            some_values = with_ones(values[unit, pl.ds(start, sub), :])
-            first = me * local_span + start
-            live = first + lax.broadcasted_iota(jnp.int32, (1, sub), 1) < length
-            scores = jnp.where(live, scores, masked_score)
+            last = item + 1 == len(items)
+            if last:
+                following = (next_unit, next_step, 0, 0)
+            else:
+                following = (unit, step) + items[item + 1]
             here = pl.ds(index * chunk, chunk)
             old = top[here, :]
-            new = jnp.maximum(old, jnp.max(scores, axis=1, keepdims=True) * scale)
-            weights = jnp.exp2(scores * scale - new[:, :1]).astype(bf16)
+            new = jnp.maximum(old, jnp.max(highest, axis=1, keepdims=True) * scale)
             factor = jnp.exp2(old - new)
             top[here, :] = new
-            acc[here, :] = acc[here, :] * jnp.concatenate([factor, factor], axis=1) + jnp.dot(
-                weights, some_values, preferred_element_type=f32
-            )
+            edge = new[:, :1]
+            mixture = acc[here, :] * jnp.concatenate([factor, factor], axis=1)
+            produced, highest = [], None
+            for tile in range(tiles):
+                scores = score_tile(*following, tile)
+                highest = lane_max(highest, scores)
+                weights = jnp.exp2(current[tile] * scale - edge).astype(bf16)
+                start = pl.multiple_of(step * block + piece * sub + tile * tile_width, tile_width)
+                mixture = mixture + jnp.dot(
+                    weights,
+                    with_ones(values[unit, pl.ds(start, tile_width), :]),
+                    preferred_element_type=f32,
+                )
+                produced.append(scores)
+            acc[here, :] = mixture
+            current = produced
+        for tile in range(tiles):
+            next_scores[:, tile * tile_width : (tile + 1) * tile_width] = current[tile]
+        next_highest[...] = highest
 
     diagonal = lax.broadcasted_iota(jnp.int32, (share, width), 0) == lax.broadcasted_iota(
         jnp.int32, (share, width), 1
@@ -236,6 +264,9 @@
 
     half = (kv_heads - 1) * group * width
 
+    load_keys(0, 0).wait()
+    prime()
+
     @pl.loop(0, units * blocks)
     def _(index):
         unit = index // blocks
@@ -249,9 +280,14 @@
         def _():
             merge(unit - 1)
 
-        load_keys(unit, step).wait()
+        following = lax.rem(index + 1, units * blocks)
+
+        @pl.when(following > 0)
+        def _():
+            load_keys(following // blocks, following % blocks).wait()
+
         load_values(unit, step).wait()
-        attend(unit, step)
+        attend(unit, step, following // blocks, following % blocks)
 
         @pl.when(step == blocks - 1)
         def _():
@@ -315,12 +351,13 @@
     tokens = batch * draft
     block = min(4096, local_span)
     sub = min(2048, block)
+    tile_width = min(1024, sub)
     blocks = local_span // block
     chunk = 320 if rows % 320 == 0 else rows
     dma = pltpu.SemaphoreType.DMA
     anywhere = pl.BlockSpec(memory_space=pl.ANY)
     return pl.pallas_call(
-        functools.partial(layer_kernel, kv_count, head_count, chunk, block, sub),
+        functools.partial(layer_kernel, kv_count, head_count, chunk, block, sub, tile_width),
         out_shape=jax.ShapeDtypeStruct((batch, draft, columns), bf16),
         in_specs=[pl.BlockSpec(memory_space=pltpu.SMEM)] + [anywhere] * 6,
         out_specs=pl.BlockSpec(memory_space=pltpu.VMEM),
@@ -333,6 +370,8 @@
             pltpu.VMEM((head_count, features, columns), bf16),
             pltpu.VMEM((rows, 2 * width), f32),
             pltpu.VMEM((rows, width), f32),
+            pltpu.VMEM((chunk, sub), f32),
+            pltpu.VMEM((chunk, width), f32),
             pltpu.VMEM((units, rows, width), bf16),
             pltpu.VMEM((units, kv_count, 8, width), f32),
             pltpu.VMEM((units, kv_count, share, width), bf16),

time: 68.7 us -> 69.3 us (level)
  no operation moved by 1% of the time
where the time goes in v3:
time: 69.3 us; the launch traced here: 69.1 us
  Pallas kernels  67.6 us (98%)
  local copies, waits for them, and re-layouts  1.53 us (2%)
    pallas_call x1, Pallas kernels, fast_per_device(): pl.pallas_call(functools.partial(layer_kernel, kv_count, head_count, chun...  67.6 us
    unnamed x1, local copies, waits for them, and re-layouts  1.53 us

profile of v3, /device:TPU:1, one launch (start us, length us, event | category | flops | bytes accessed | tf_op | source)
XLA Modules:
  0.0 69.1 jit_solution(9252687492930497576)
XLA Ops:
  0.0 67.6 %shard_map.73 = bf16[2,40,512]{2,1,0:T(8,128)(2,1)} custom-call(s32[2]{0:T(128)} %lengths_ref.1, bf16[2,40,32,128]{3,2,1,0:T(8,128)(2,1)} %q_hbm.1, bf16[2,2,8192,128]{3,2,1,0:T(8,128)(2,1)} %k_hbm.1, bf16[2,2,8192,128]{3,2,1,0:T(8,128)(2,1)} %v_hbm.1, bf16[2,2,40,128]{3,2,1,0:T(8,128)(2,1)} %dk_hbm.1, bf16[2,2,40,128]{3,2,1,0:T(8,128)(2,1)} %dv_hbm.1, ...), custom_call_target="tpu_custom_call" | custom-call | flops 12079595520 | bytes 33554432 | tf_op jit(solution)/shard_map/pallas_call | solution.py:359
  67.6 1.5 %copy.9 = bf16[2,40,512]{2,1,0:T(8,128)(2,1)} copy(bf16[2,40,512]{2,1,0:T(8,128)(2,1)} %shard_map.73) | data formatting | bytes 163840

commit v4 on v2

--- a/solution.py
+++ b/solution.py
@@ -170,7 +170,7 @@
             some_values = with_ones(values[unit, pl.ds(start, sub), :])
             first = me * local_span + start
             live = first + lax.broadcasted_iota(jnp.int32, (1, sub), 1) < length
-            scores = jnp.where(live, scores, masked_score)
+            scores = scores + jnp.where(live, 0.0, masked_score)
             here = pl.ds(index * chunk, chunk)
             old = top[here, :]
             new = jnp.maximum(old, jnp.max(scores, axis=1, keepdims=True) * scale)

time: 68.7 us -> 70.6 us (1.028)
  Pallas kernels: 67 us -> 68.9 us
    pallas_call x1, Pallas kernels: 67 us -> 68.9 us  [fast_per_device(): pl.pallas_call(functools.partial(layer_kernel, kv_count, head_count, chun...]
where the time goes in v4:
time: 70.6 us; the launch traced here: 70.4 us
  Pallas kernels  68.9 us (98%)
  local copies, waits for them, and re-layouts  1.53 us (2%)
    pallas_call x1, Pallas kernels, fast_per_device(): pl.pallas_call(functools.partial(layer_kernel, kv_count, head_count, chun...  68.9 us
    unnamed x1, local copies, waits for them, and re-layouts  1.53 us

profile of v4, /device:TPU:1, one launch (start us, length us, event | category | flops | bytes accessed | tf_op | source)
XLA Modules:
  0.0 70.4 jit_solution(11964158019231893767)
XLA Ops:
  0.0 68.9 %shard_map.73 = bf16[2,40,512]{2,1,0:T(8,128)(2,1)} custom-call(s32[2]{0:T(128)} %lengths_ref.1, bf16[2,40,32,128]{3,2,1,0:T(8,128)(2,1)} %q_hbm.1, bf16[2,2,8192,128]{3,2,1,0:T(8,128)(2,1)} %k_hbm.1, bf16[2,2,8192,128]{3,2,1,0:T(8,128)(2,1)} %v_hbm.1, bf16[2,2,40,128]{3,2,1,0:T(8,128)(2,1)} %dk_hbm.1, bf16[2,2,40,128]{3,2,1,0:T(8,128)(2,1)} %dv_hbm.1, ...), custom_call_target="tpu_custom_call" | custom-call | flops 12079595520 | bytes 33554432 | tf_op jit(solution)/shard_map/pallas_call | solution.py:322
  68.9 1.5 %copy.9 = bf16[2,40,512]{2,1,0:T(8,128)(2,1)} copy(bf16[2,40,512]{2,1,0:T(8,128)(2,1)} %shard_map.73) | data formatting | bytes 163840
